TPU v7x, 32 devices: a whole 2x2x4 slice. The times are simulated.
32 devices in a mesh: tok: 8 (over y, x, core), wid: 4 (over z).
Axes of the slice: x: 2, y: 2, z: 4, core: 2. Of those that a mesh axis runs over, the one named last changes fastest.
Arguments:
- patches: bfloat16 [1536, 8, 6144], P('tok', None, 'wid'), may hold values from -6 to 6
- w_query: bfloat16 [6144, 4096], P('tok', 'wid'), may hold values from -0.102062073 to 0.102062073
- w_key: bfloat16 [6144, 4096], P('tok', 'wid'), may hold values from -0.102062073 to 0.102062073
- w_value: bfloat16 [6144, 4096], P('tok', 'wid'), may hold values from -0.078125 to 0.078125
- q_gain: float32 [4096], P('wid'), may hold values from 0.5 to 6
- k_gain: float32 [4096], P('wid'), may hold values from 0.5 to 6
- w_out: bfloat16 [4096, 6144], P('tok', 'wid'), may hold values from -0.09375 to 0.09375
Outputs:
- layer_out: bfloat16 [1536, 8, 6144], P('tok', None, 'wid')
All inputs are finite; a program needn't handle non-finite values.
Results may differ from a plain program's by a relative error of at most 0.0034.
The roundings to bfloat16 on the way count: a program that leaves them out, or rounds other values in their place, can miss the bound.
Values may be sent and summed in bfloat16 or wider, within the bound.
A program may use at most 192 MiB of HBM per device.

v0:
```python
import jax
import jax.numpy as jnp
from jax import lax
from jax.sharding import PartitionSpec as P

D = 6144
HEAD_DIM = 128
HD = 4096


def layer_norm_rows(values, eps):
    mean = jnp.mean(values, axis=-1, keepdims=True)
    var = jnp.mean(values * values, axis=-1, keepdims=True) - mean * mean
    return (values - mean) * lax.rsqrt(var + eps)


def add_rows(left, piece):
    return jnp.dot(left, piece, preferred_element_type=jnp.float32)


def head_norm(values, gain, eps):
    rows, images, width = values.shape
    heads_here = width // HEAD_DIM
    shaped = values.reshape(rows, images, heads_here, HEAD_DIM)
    normed = layer_norm_rows(shaped, eps) * gain.reshape(heads_here, HEAD_DIM)
    return normed.astype(jnp.bfloat16).reshape(rows, images * heads_here, HEAD_DIM)


def local(patches, w_query, w_key, w_value, q_gain, k_gain, w_out):
    local_rows, images, local_width = patches.shape
    as_float = patches.astype(jnp.float32)
    totals = lax.psum((jnp.sum(as_float, axis=-1), jnp.sum(as_float * as_float, axis=-1)), "wid")
    mean = totals[0] / D
    var = totals[1] / D - mean * mean
    normed = ((as_float - mean[..., None]) * lax.rsqrt(var + 1e-06)[..., None]).astype(jnp.bfloat16)
    whole = lax.all_gather(normed, "wid", axis=2, tiled=True)
    flat = whole.reshape(local_rows * images, D)

    def add_one(piece):
        return add_rows(flat, piece)

    query = add_one(lax.all_gather(w_query, "tok", axis=0, tiled=True))
    key = add_one(lax.all_gather(w_key, "tok", axis=0, tiled=True))
    value = add_one(lax.all_gather(w_value, "tok", axis=0, tiled=True))
    head_width = query.shape[1]
    heads_here = head_width // HEAD_DIM
    qnorm = head_norm(query.reshape(local_rows, images, head_width), q_gain, 1e-06)
    knorm = head_norm(key.reshape(local_rows, images, head_width), k_gain, 1e-06)
    vshaped = value.astype(jnp.bfloat16).reshape(local_rows, images * heads_here, HEAD_DIM)
    qfull, kfull, vfull = (
        lax.all_to_all(qnorm, "tok", split_axis=1, concat_axis=0, tiled=True),
        lax.all_to_all(knorm, "tok", split_axis=1, concat_axis=0, tiled=True),
        lax.all_to_all(vshaped, "tok", split_axis=1, concat_axis=0, tiled=True),
    )
    seq_rows, item_count, _ = qfull.shape
    block = min(512, seq_rows)
    blocks = qfull.reshape(seq_rows // block, block, item_count, HEAD_DIM)
    scale = HEAD_DIM ** (-0.5)

    def attend(qblock):
        scores = (
            jnp.einsum("qid,kid->iqk", qblock, kfull, preferred_element_type=jnp.float32) * scale
        )
        top = jnp.max(scores, axis=-1, keepdims=True)
        expo = jnp.exp(scores - top)
        probs = (expo / jnp.sum(expo, axis=-1, keepdims=True)).astype(jnp.bfloat16)
        return jnp.einsum("iqk,kid->qid", probs, vfull, preferred_element_type=jnp.float32).astype(
            jnp.bfloat16
        )

    attended = lax.map(attend, blocks).reshape(seq_rows, item_count, HEAD_DIM)
    returned = lax.all_to_all(attended, "tok", split_axis=0, concat_axis=1, tiled=True)
    mixed = returned.reshape(local_rows, images, head_width)
    mixed_whole = lax.all_gather(mixed, "wid", axis=2, tiled=True).reshape(local_rows * images, HD)
    branch = add_rows(mixed_whole, lax.all_gather(w_out, "tok", axis=0, tiled=True))
    return (as_float + branch.reshape(local_rows, images, local_width)).astype(jnp.bfloat16)


def solution(mesh):
    placed = (
        P("tok", None, "wid"),
        P("tok", "wid"),
        P("tok", "wid"),
        P("tok", "wid"),
        P("wid"),
        P("wid"),
        P("tok", "wid"),
    )
    return jax.shard_map(
        local, mesh=mesh, in_specs=placed, out_specs=P("tok", None, "wid"), check_vma=False
    )
```

profile of v0, /device:TPU:0, one launch (start us, length us, event | category | flops | bytes accessed | tf_op | source)
XLA Modules:
  0.0 1095.7 jit_solution(18060111817677011343)
XLA Ops:
  8.1 3.9 convert_reduce_fusion
  12.1 20.5 %all-reduce = (f32[192,8]{0,1:T(8,128)S(1)}, f32[192,8]{0,1:T(8,128)S(1)}) all-reduce(f32[192,8]{0,1:T(8,128)S(1)} %copy.85, f32[192,8]{0,1:T(8,128)S(1)} %copy.83), channel_id=1, replica_groups=mesh['tok'=8,'wid'=4] {'wid'}, use_global_device_ids=true, to_apply=%region_3.0 | all-reduce | flops 3072 | bytes 24576 | tf_op jit(solution)/shard_map/psum | solution.py:32
  32.9 5.7 fusion.26
  39.7 44.4 %all-gather.11.cloned.1.call-done = bf16[6144,1024]{1,0:T(8,128)(2,1)} async-done(((bf16[768,1024]{1,0:T(8,128)(2,1)}), bf16[6144,1024]{1,0:T(8,128)(2,1)}) %all-gather.11.cloned.1.call-update) | async-done | bytes 12582928 | tf_op jit(solution)/shard_map/all_gather | solution.py:43
  84.1 16.9 %copy.96 = bf16[1024,6144]{1,0:T(8,128)(2,1)} copy(bf16[1024,6144]{0,1:T(8,128)(2,1)} %bitcast.93) | data formatting | bytes 25165824 | tf_op jit(solution)/shard_map/dot_general | solution.py:18
  101.0 57.1 %all-gather.9.cloned.1.call-done = bf16[6144,1024]{1,0:T(8,128)(2,1)} async-done(((bf16[768,1024]{1,0:T(8,128)(2,1)}), bf16[6144,1024]{1,0:T(8,128)(2,1)}) %all-gather.9.cloned.1.call-update) | async-done | bytes 12582928 | tf_op jit(solution)/shard_map/all_gather | solution.py:42
  158.2 17.2 %copy.87 = bf16[1024,6144]{1,0:T(8,128)(2,1)} copy(bf16[1024,6144]{0,1:T(8,128)(2,1)} %bitcast.94) | data formatting | bytes 25165824 | tf_op jit(solution)/shard_map/dot_general | solution.py:18
  175.4 307.0 %all-gather.7.cloned.1.call-done = bf16[192,8,6144]{2,1,0:T(8,128)(2,1)} async-done(((bf16[192,8,1536]{2,1,0:T(8,128)(2,1)}), bf16[192,8,6144]{2,1,0:T(8,128)(2,1)}) %all-gather.7.cloned.1.call-update) | async-done | bytes 18874384 | tf_op jit(solution)/shard_map/all_gather | solution.py:36
  482.4 30.5 %fusion.34 = (f32[192,8,8]{1,2,0:T(8,128)S(1)}, f32[192,8,8]{1,2,0:T(8,128)S(1)}, f32[192,8,8,128]{3,1,2,0:T(8,128)}) fusion(bf16[8,128,6144,1]{2,1,0,3:T(8,128)(2,1)} %bitcast.96, bf16[192,8,6144]{2,1,0:T(8,128)(2,1)} %all-gather.7.cloned.1.call-done), kind=kOutput, calls=%fused_computation.47 | convolution fusion | flops 19332046848 | bytes 37847040 | tf_op jit(solution)/shard_map/dot_general | solution.py:18
  514.3 7.7 multiply_convert_fusion
  526.4 5.1 all-to-all-start.1
  531.5 30.8 %fusion.35 = (f32[192,8,8]{1,2,0:T(8,128)S(1)}, f32[192,8,8]{1,2,0:T(8,128)S(1)}, f32[192,8,8,128]{3,1,2,0:T(8,128)}) fusion(bf16[8,128,6144,1]{2,1,0,3:T(8,128)(2,1)} %bitcast.95, bf16[192,8,6144]{2,1,0:T(8,128)(2,1)} %all-gather.7.cloned.1.call-done), kind=kOutput, calls=%fused_computation.48 | convolution fusion | flops 19332046848 | bytes 37847040 | tf_op jit(solution)/shard_map/dot_general | solution.py:18
  563.7 7.2 multiply_convert_fusion.1
  575.4 12.1 %all-to-all-done.1 = bf16[192,64,128]{2,0,1:T(8,128)(2,1)} async-done(((bf16[192,64,128]{2,0,1:T(8,128)(2,1)}), bf16[192,64,128]{2,0,1:T(8,128)(2,1)}, u32[]{:S(2)}, u32[]{:S(2)}) %all-to-all-start.1) | async-done | bytes 3145760 | tf_op jit(solution)/shard_map/all_to_all | solution.py:52
  591.4 27.2 %fusion.31 = bf16[1536,1024]{1,0:T(8,128)(2,1)} fusion(bf16[6144,1024]{1,0:T(8,128)(2,1)} %all-gather.13.cloned.1.call-done, bf16[192,8,6144]{2,1,0:T(8,128)(2,1)} %all-gather.7.cloned.1.call-done), kind=kOutput, calls=%fused_computation.37 | convolution fusion | flops 19328925696 | bytes 34603008 | tf_op jit(solution)/shard_map/dot_general | solution.py:18
  618.7 5.8 reshape.79
  624.5 5.6 copy.105
  630.1 15.9 %all-to-all-done = bf16[192,64,128]{2,0,1:T(8,128)(2,1)S(1)} async-done(((bf16[192,64,128]{2,0,1:T(8,128)(2,1)}), bf16[192,64,128]{2,0,1:T(8,128)(2,1)S(1)}, u32[]{:S(2)}, u32[]{:S(2)}) %all-to-all-start) | async-done | bytes 3145760 | tf_op jit(solution)/shard_map/all_to_all | solution.py:51
  646.0 4.4 all-to-all-start.2
  650.5 4.9 copy.104
  661.3 59.8 %all-to-all-done.2 = bf16[192,64,128]{2,0,1:T(8,128)(2,1)} async-done(((bf16[192,64,128]{2,0,1:T(8,128)(2,1)}), bf16[192,64,128]{2,0,1:T(8,128)(2,1)}, u32[]{:S(2)}, u32[]{:S(2)}) %all-to-all-start.2) | async-done | bytes 3145760 | tf_op jit(solution)/shard_map/all_to_all | solution.py:53
  725.0 72.1 %while.10 = (s32[]{:T(128)}, bf16[3,512,8,128]{3,2,1,0:T(8,128)(2,1)}, bf16[3,512,8,128]{3,2,1,0:T(8,128)(2,1)}, bf16[1536,8,128]{2,0,1:T(8,128)(2,1)}, bf16[1536,8,128]{2,0,1:T(8,128)(2,1)}, /*index=5*/s32[]{:T(128)}) while((s32[]{:T(128)}, bf16[3,512,8,128]{3,2,1,0:T(8,128)(2,1)}, bf16[3,512,8,128]{3,2,1,0:T(8,128)(2,1)}, ...), condition=%wide.region_11.12_spmd, body=%wide.region_8.11_spmd.sunk | while | flops 4876409856 | bytes 16810568 | solution.py:71
  726.5 9.0 fusion.54
  735.5 12.0 %fusion.55 = bf16[1,512,8,128]{3,1,2,0:T(8,128)(2,1)S(1)} fusion(bf16[1536,8,128]{2,0,1:T(8,128)(2,1)} %get-tuple-element.136, f32[8,512]{1,0:T(8,128)S(1)} %fusion.54, bf16[1536,8,128]{2,0,1:T(8,128)(2,1)} %get-tuple-element.135, bf16[1,512,8,128]{3,2,1,0:T(8,128)(2,1)S(1)} %constant_dynamic-slice_fusion.2), kind=kOutput, calls=%fused_computation.9.clone.1 | convolution fusion | flops 3246921216 | bytes 8404992 | tf_op jit(solution)/shard_map/while/body/eval_jaxpr/iqk,kid->qid/dot_general | solution.py:67
  750.5 9.0 fusion.54
  759.5 12.0 %fusion.55 = bf16[1,512,8,128]{3,1,2,0:T(8,128)(2,1)S(1)} fusion(bf16[1536,8,128]{2,0,1:T(8,128)(2,1)} %get-tuple-element.136, f32[8,512]{1,0:T(8,128)S(1)} %fusion.54, bf16[1536,8,128]{2,0,1:T(8,128)(2,1)} %get-tuple-element.135, bf16[1,512,8,128]{3,2,1,0:T(8,128)(2,1)S(1)} %constant_dynamic-slice_fusion.2), kind=kOutput, calls=%fused_computation.9.clone.1 | convolution fusion | flops 3246921216 | bytes 8404992 | tf_op jit(solution)/shard_map/while/body/eval_jaxpr/iqk,kid->qid/dot_general | solution.py:67
  774.4 9.0 fusion.54
  783.4 12.0 %fusion.55 = bf16[1,512,8,128]{3,1,2,0:T(8,128)(2,1)S(1)} fusion(bf16[1536,8,128]{2,0,1:T(8,128)(2,1)} %get-tuple-element.136, f32[8,512]{1,0:T(8,128)S(1)} %fusion.54, bf16[1536,8,128]{2,0,1:T(8,128)(2,1)} %get-tuple-element.135, bf16[1,512,8,128]{3,2,1,0:T(8,128)(2,1)S(1)} %constant_dynamic-slice_fusion.2), kind=kOutput, calls=%fused_computation.9.clone.1 | convolution fusion | flops 3246921216 | bytes 8404992 | tf_op jit(solution)/shard_map/while/body/eval_jaxpr/iqk,kid->qid/dot_general | solution.py:67
  797.1 41.6 %all_to_all.66 = bf16[1536,8,128]{2,1,0:T(8,128)(2,1)S(1)} all-to-all(bf16[1536,8,128]{2,1,0:T(8,128)(2,1)} %bitcast.104), channel_id=1, replica_groups=mesh['tok'=8,'wid'=4] {'tok'}, dimensions={0} | all-to-all | bytes 6291456 | tf_op jit(solution)/shard_map/all_to_all | solution.py:72
  838.7 5.3 copy.133
  844.1 217.4 %all-gather.15.cloned.1.call-done = bf16[192,8,4096]{2,1,0:T(8,128)(2,1)} async-done(((bf16[192,8,1024]{2,1,0:T(8,128)(2,1)}), bf16[192,8,4096]{2,1,0:T(8,128)(2,1)}) %all-gather.15.cloned.1.call-update) | async-done | bytes 12582928 | tf_op jit(solution)/shard_map/all_gather | solution.py:74
  1061.5 27.1 %fusion.28 = bf16[192,8,1536]{2,1,0:T(8,128)(2,1)} fusion(bf16[192,8,1536]{2,1,0:T(8,128)(2,1)} %param.9, bf16[192,8,4096]{2,1,0:T(8,128)(2,1)} %all-gather.15.cloned.1.call-done, bf16[4096,1536]{1,0:T(8,128)(2,1)} %all-gather.17.cloned.1.call-done), kind=kOutput, calls=%fused_computation.32 | convolution fusion | flops 19334430720 | bytes 34603008 | tf_op jit(solution)/shard_map/dot_general | solution.py:18
  (48 shorter events, 37.4 us)
Async XLA Ops:
  6.5 77.6 %all-gather.11.cloned.1.call-start = ((), (), s32[]{:S(2)}) async-start(), calls=%async_computation.6 | async-start | bytes 14155776 | tf_op jit(solution)/shard_map/all_gather | solution.py:43
  7.3 150.9 %all-gather.9.cloned.1.call-start = ((), (), s32[]{:S(2)}) async-start(), calls=%async_computation.5 | async-start | bytes 14155776 | tf_op jit(solution)/shard_map/all_gather | solution.py:42
  8.0 474.4 %all-gather.7.cloned.1.call-start = ((), (), s32[]{:S(2)}) async-start(), calls=%async_computation.4 | async-start | bytes 23592960 | tf_op jit(solution)/shard_map/all_gather | solution.py:36
  38.6 552.8 %all-gather.13.cloned.1.call-start = ((), (), s32[]{:S(2)}) async-start(), calls=%async_computation.7 | async-start | bytes 14155776 | tf_op jit(solution)/shard_map/all_gather | solution.py:44
  39.1 805.0 %all-gather.17.cloned.1.call-start = ((), (), s32[]{:S(2)}) async-start(), calls=%async_computation.9 | async-start | bytes 14155776 | tf_op jit(solution)/shard_map/all_gather | solution.py:75
  482.4 31.9 %copy-start = (f32[1024]{0:T(1024)S(1)}, f32[1024]{0:T(1024)}, u32[]{:S(2)}) copy-start(f32[1024]{0:T(1024)} %param.14) | copy-start | bytes 12292
  526.4 61.1 %all-to-all-start.1 = ((bf16[192,64,128]{2,0,1:T(8,128)(2,1)}), bf16[192,64,128]{2,0,1:T(8,128)(2,1)}, u32[]{:S(2)}, u32[]{:S(2)}) async-start(bf16[192,64,128]{2,0,1:T(8,128)(2,1)} %copy.102), calls=%async_computation.1 | async-start | bytes 6291456 | tf_op jit(solution)/shard_map/all_to_all | solution.py:52
  531.5 32.2 %copy-start.1 = (f32[1024]{0:T(1024)S(1)}, f32[1024]{0:T(1024)}, u32[]{:S(2)}) copy-start(f32[1024]{0:T(1024)} %param.13) | copy-start | bytes 12292
  587.5 58.4 %all-to-all-start = ((bf16[192,64,128]{2,0,1:T(8,128)(2,1)}), bf16[192,64,128]{2,0,1:T(8,128)(2,1)S(1)}, u32[]{:S(2)}, u32[]{:S(2)}) async-start(bf16[192,64,128]{2,0,1:T(8,128)(2,1)} %copy.93), calls=%async_computation | async-start | bytes 6291456 | tf_op jit(solution)/shard_map/all_to_all | solution.py:51
  646.0 75.2 %all-to-all-start.2 = ((bf16[192,64,128]{2,0,1:T(8,128)(2,1)}), bf16[192,64,128]{2,0,1:T(8,128)(2,1)}, u32[]{:S(2)}, u32[]{:S(2)}) async-start(bf16[192,64,128]{2,0,1:T(8,128)(2,1)} %copy.105), calls=%async_computation.2 | async-start | bytes 6291456 | tf_op jit(solution)/shard_map/all_to_all | solution.py:53
  650.4 411.1 %all-gather.15.cloned.1.call-start = ((), (), s32[]{:S(2)}) async-start(), calls=%async_computation.8 | async-start | bytes 15728640 | tf_op jit(solution)/shard_map/all_gather | solution.py:74
Sparse Core Ops, SparseCore 0:
  9.2 74.8 all-gather.10
  86.0 72.1 all-gather.8
  159.7 322.5 all-gather.6
  484.1 96.2 all-gather.12
  582.1 139.2 all-gather.16
  844.2 217.2 all-gather.14
where the time goes:
time: 1100 us
  waiting for transfers between devices  716 us (65%)
  matrix products  179 us (16%)
  local copies, waits for them, and re-layouts  86.4 us (8%)
  blocking collectives  62.1 us (6%)
  other arithmetic  24.5 us (2%)
  between operations  13.9 us (1%)
  starting transfers between devices  13.8 us (1%)
    all_gather x1, waiting for transfers between devices, local(): whole = lax.all_gather(normed, 'wid', axis=2, tiled=True)  307 us
    all_gather x1, waiting for transfers between devices, local(): lax.all_gather(mixed, 'wid', axis=2, tiled=True)  217 us
    dot_general x4, matrix products, add_rows(): return jnp.dot(left, piece, preferred_element_type=jnp.float32)  116 us
    all_to_all x1, waiting for transfers between devices, local(): lax.all_to_all(vshaped, 'tok', split_axis=1, concat_axis=0, tiled=True)  59.8 us
    all_gather x1, waiting for transfers between devices, local(): query = add_one(lax.all_gather(w_query, 'tok', axis=0, tiled=True))  57.1 us
    all_gather x1, waiting for transfers between devices, local(): key = add_one(lax.all_gather(w_key, 'tok', axis=0, tiled=True))  44.4 us
    all_to_all x1, blocking collectives, local(): lax.all_to_all(attended, 'tok', split_axis=0, concat_axis=1, tiled=True)  41.6 us
    dot_general x3, matrix products, attend(): jnp.einsum('iqk,kid->qid', probs, vfull, preferred_element_type=jnp.float32)  36 us
  transfers between devices with their start and end apart: 9, of which 7 were waited for; matrix products, arithmetic and copies ran while one was open for 24% of the time, Pallas kernels for 0%

commit v1 on v0

v1 whole, which is shorter than its diff:
```python
import jax
import jax.numpy as jnp
from jax import lax
from jax.experimental import pallas as pl
from jax.experimental.pallas import tpu as pltpu
from jax.sharding import PartitionSpec as P

HEAD_DIM = 128
EPS = 1e-06


def layer_norm_rows(values, eps):
    mean = jnp.mean(values, axis=-1, keepdims=True)
    var = jnp.mean(values * values, axis=-1, keepdims=True) - mean * mean
    return (values - mean) * lax.rsqrt(var + eps)


def xor_gather(block, axis, count, order):
    keys = [0]
    data = block[None]
    pieces = {0: (data, 0)}
    for bit in order:
        step = 1 << bit
        got = lax.ppermute(data, axis, [(i, i ^ step) for i in range(count)])
        for slot, key in enumerate(keys):
            pieces[key ^ step] = (got, slot)
        keys = keys + [key ^ step for key in keys]
        if len(keys) < count:
            data = jnp.concatenate([data, got], axis=0)
    return [pieces[j][0][pieces[j][1]] for j in range(count)]


def gather_rows(weight, axis, count):
    bits = count.bit_length() - 1
    half = weight.shape[0] // 2
    first = xor_gather(weight[:half], axis, count, list(range(1, bits)) + [0])
    second = xor_gather(weight[half:], axis, count, list(range(bits - 1, 0, -1)) + [0])
    return jnp.concatenate([x for pair in zip(first, second) for x in pair], axis=0)


def xor_columns(whole, me, count):
    parts, columns = whole.shape[0], whole.shape[-1]
    per = count // parts
    width = columns // per
    sizes = (1,) + whole.shape[1:-1] + (width,)
    blocks = []
    for j in range(count):
        b = me ^ j
        start = (b // per,) + (0,) * (whole.ndim - 2) + ((b % per) * width,)
        blocks.append(lax.dynamic_slice(whole, start, sizes)[0])
    return blocks


def attend_kernel(q_ref, k_ref, v_ref, o_ref):
    near = (((1,), (1,)), ((), ()))
    far = (((1,), (0,)), ((), ()))
    q = q_ref[...].reshape(-1, HEAD_DIM)
    k = k_ref[...].reshape(-1, HEAD_DIM)
    v = v_ref[...].reshape(-1, HEAD_DIM)
    scores = lax.dot_general(q, k, near, preferred_element_type=jnp.float32) * HEAD_DIM ** (-0.5)
    expo = jnp.exp(scores - jnp.max(scores, axis=-1, keepdims=True))
    probs = (expo * (1.0 / jnp.sum(expo, axis=-1, keepdims=True))).astype(jnp.bfloat16)
    mixed = lax.dot_general(probs, v, far, preferred_element_type=jnp.float32)
    o_ref[...] = mixed.astype(jnp.bfloat16).reshape(o_ref.shape)


def attend(full):
    toks, items, _, rows, _ = full.shape
    step = max(1, 384 // rows)
    tall = toks * rows
    return pl.pallas_call(
        attend_kernel,
        grid=(items, toks // step),
        in_specs=[
            pl.BlockSpec((step, None, None, rows, HEAD_DIM), lambda i, t: (t, i, 0, 0, 0)),
            pl.BlockSpec((toks, None, None, rows, HEAD_DIM), lambda i, t: (0, i, 1, 0, 0)),
            pl.BlockSpec((toks, None, None, rows, HEAD_DIM), lambda i, t: (0, i, 2, 0, 0)),
        ],
        out_specs=pl.BlockSpec((step, None, rows, HEAD_DIM), lambda i, t: (t, i, 0, 0)),
        out_shape=jax.ShapeDtypeStruct((toks, items, rows, HEAD_DIM), jnp.bfloat16),
        compiler_params=pltpu.CompilerParams(vmem_limit_bytes=32 * 1024 * 1024),
        cost_estimate=pl.CostEstimate(
            flops=4 * items * tall * tall * HEAD_DIM,
            bytes_accessed=8 * items * tall * HEAD_DIM,
            transcendentals=items * tall * tall,
        ),
        name="attend",
    )(full, full, full)


def solution(mesh):
    toks, wids = mesh.shape["tok"], mesh.shape["wid"]

    def local(patches, w_query, w_key, w_value, q_gain, k_gain, w_out):
        rows, images, local_width = patches.shape
        me = lax.axis_index("tok")
        head_width = w_query.shape[1]
        heads = head_width // HEAD_DIM
        model = local_width * wids
        group = max(2, toks // heads)
        groups = images // group
        items = group * heads // toks

        mine = [
            jnp.transpose(patches[:, g * group : (g + 1) * group], (1, 0, 2)) for g in range(groups)
        ]
        wholes = [lax.all_gather(m, "wid", axis=0, tiled=False) for m in mine]
        w_in = gather_rows(jnp.concatenate([w_query, w_key, w_value], axis=1), "tok", toks)
        w_last = gather_rows(w_out, "tok", toks)

        outs = []
        for g in range(groups):
            whole = wholes[g]
            as_float = whole.astype(jnp.float32)
            mean = jnp.sum(as_float, axis=(0, 3)) / model
            var = jnp.sum(as_float * as_float, axis=(0, 3)) / model - mean * mean
            inv = lax.rsqrt(var + EPS)
            normed = jnp.concatenate(
                [
                    ((b.astype(jnp.float32) - mean[..., None]) * inv[..., None]).astype(jnp.bfloat16)
                    for b in xor_columns(whole, me, toks)
                ],
                axis=-1,
            ).reshape(group * rows, model)
            qkv = jnp.dot(normed, w_in, preferred_element_type=jnp.float32)
            qkv = qkv.reshape(group, rows, 3, heads, HEAD_DIM)
            qn = (layer_norm_rows(qkv[:, :, 0], EPS) * q_gain.reshape(heads, HEAD_DIM)).astype(jnp.bfloat16)
            kn = (layer_norm_rows(qkv[:, :, 1], EPS) * k_gain.reshape(heads, HEAD_DIM)).astype(jnp.bfloat16)
            vb = qkv[:, :, 2].astype(jnp.bfloat16)
            packed = jnp.stack([qn, kn, vb], axis=0)
            packed = jnp.transpose(packed, (1, 3, 0, 2, 4)) if heads < toks else jnp.transpose(packed, (3, 1, 0, 2, 4))
            packed = packed.reshape(toks, items, 3, rows, HEAD_DIM)
            full = lax.all_to_all(packed, "tok", split_axis=0, concat_axis=0, tiled=False)
            back = lax.all_to_all(attend(full), "tok", split_axis=0, concat_axis=0, tiled=False)
            if heads < toks:
                back = jnp.transpose(back.reshape(group, heads, rows, HEAD_DIM), (0, 2, 1, 3))
            else:
                back = jnp.transpose(back.reshape(heads, group, rows, HEAD_DIM), (1, 2, 0, 3))
            mixed = back.reshape(group * rows, head_width)
            every = lax.all_gather(mixed, "wid", axis=0, tiled=False)
            every = jnp.concatenate(xor_columns(every, me, toks), axis=-1)
            branch = jnp.dot(every, w_last, preferred_element_type=jnp.float32)
            out = mine[g].astype(jnp.float32) + branch.reshape(group, rows, local_width)
            outs.append(jnp.transpose(out.astype(jnp.bfloat16), (1, 0, 2)))
        return jnp.concatenate(outs, axis=1)

    placed = (
        P("tok", None, "wid"),
        P("tok", "wid"),
        P("tok", "wid"),
        P("tok", "wid"),
        P("wid"),
        P("wid"),
        P("tok", "wid"),
    )
    return jax.shard_map(
        local, mesh=mesh, in_specs=placed, out_specs=P("tok", None, "wid"), check_vma=False
    )
```

time: 1100 us -> 939 us (0.85)
  waiting for transfers between devices: 716 us -> 369 us
  local copies, waits for them, and re-layouts: 86.4 us -> 198 us
  other arithmetic: 24.5 us -> 118 us
  Pallas kernels: 0 us -> 67.1 us
  blocking collectives: 62.1 us -> 0 us
  matrix products: 179 us -> 119 us
  starting transfers between devices: 13.8 us -> 43 us
    all_gather x6 -> x8, waiting for transfers between devices: 626 us -> 107 us  [the longest x4 91.9 us: local(): wholes = [lax.all_gather(m, 'wid', axis=0, tiled=False) for m in mine]]
    ppermute x0 -> x12, waiting for transfers between devices: none -> 190 us  [xor_gather(): got = lax.ppermute(data, axis, [(i, i ^ step) for i in range(count)])]
    unnamed x4 -> x149, local copies, waits for them, and re-layouts: 0.01 us -> 111 us
    pallas_call x0 -> x4, Pallas kernels: none -> 67.1 us  [attend(): pl.pallas_call(attend_kernel, grid=(items, toks // step), in_specs=[pl.Bl...]
    all_to_all x1 -> x0, blocking collectives: 41.6 us -> none  [local(): lax.all_to_all(attended, 'tok', split_axis=0, concat_axis=1, tiled=True)]
    unnamed x0 -> x29, other arithmetic: none -> 35.7 us
    concatenate x0 -> x13, other arithmetic: none -> 34 us  [the longest x8 28.4 us: xor_gather(): data = jnp.concatenate([data, got], axis=0)]
    dot_general x7 -> x8, matrix products: 152 us -> 119 us  [the longest x4 82 us: local(): qkv = jnp.dot(normed, w_in, preferred_element_type=jnp.float32)]
  transfers between devices with their start and end apart: 9 -> 28, of which waited for: 7 -> 12; matrix products, arithmetic and copies ran while one was open for 24% -> 42% of each run, Pallas kernels for 0% -> 7%
where the time goes in v1:
time: 939 us; the launch traced here: 929 us
  waiting for transfers between devices  369 us (39%)
  local copies, waits for them, and re-layouts  198 us (21%)
  matrix products  119 us (13%)
  other arithmetic  118 us (13%)
  Pallas kernels  67.1 us (7%)
  starting transfers between devices  43 us (5%)
  between operations  15 us (2%)
    ppermute x12, waiting for transfers between devices, xor_gather(): got = lax.ppermute(data, axis, [(i, i ^ step) for i in range(count)])  190 us
    unnamed x149, local copies, waits for them, and re-layouts  111 us
    all_gather x4, waiting for transfers between devices, local(): wholes = [lax.all_gather(m, 'wid', axis=0, tiled=False) for m in mine]  91.9 us
    dot_general x4, matrix products, local(): qkv = jnp.dot(normed, w_in, preferred_element_type=jnp.float32)  82 us
    pallas_call x4, Pallas kernels, attend(): pl.pallas_call(attend_kernel, grid=(items, toks // step), in_specs=[pl.Bl...  67.1 us
    all_to_all x4, waiting for transfers between devices, local(): lax.all_to_all(packed, 'tok', split_axis=0, concat_axis=0, tiled=False)  54.7 us
    dot_general x1, local copies, waits for them, and re-layouts, local(): qkv = jnp.dot(normed, w_in, preferred_element_type=jnp.float32)  48.6 us
    dot_general x4, matrix products, local(): branch = jnp.dot(every, w_last, preferred_element_type=jnp.float32)  37.3 us
  transfers between devices with their start and end apart: 28, of which 12 were waited for; matrix products, arithmetic and copies ran while one was open for 42% of the time, Pallas kernels for 7%

profile of v1, /device:TPU:0, one launch (start us, length us, event | category | flops | bytes accessed | tf_op | source)
XLA Modules:
  0.0 929.4 jit_solution(7696079984090109226)
XLA Ops:
  6.5 12.1 %fusion.164 = (bf16[192,2,1536]{2,1,0:T(2,128)(2,1)S(1)}, bf16[192,2,1536]{2,1,0:T(2,128)(2,1)S(1)}, bf16[192,2,1536]{2,1,0:T(2,128)(2,1)}, bf16[192,2,1536]{2,1,0:T(2,128)(2,1)S(1)}) fusion(bf16[192,8,1536]{2,1,0:T(8,128)(2,1)} %param.7), kind=kLoop, calls=%fused_computation.348 | loop fusion | bytes 9437184 | tf_op jit(solution)/shard_map/slice | solution.py:105
  34.6 49.7 %collective-permute-done = bf16[1,384,3072]{2,1,0:T(8,128)(2,1)S(1)} collective-permute-done((bf16[1,384,3072]{2,1,0:T(8,128)(2,1)S(1)}, bf16[1,384,3072]{2,1,0:T(8,128)(2,1)S(1)}, u32[]{:S(2)}, u32[]{:S(2)}) %collective-permute-start) | collective-permute-done | bytes 2359328 | tf_op jit(solution)/shard_map/ppermute | solution.py:24
  95.1 116.9 %collective-permute-done.6 = bf16[1,256,1536]{2,1,0:T(8,128)(2,1)S(1)} collective-permute-done((bf16[1,256,1536]{2,1,0:T(8,128)(2,1)S(1)}, bf16[1,256,1536]{2,1,0:T(8,128)(2,1)S(1)}, u32[]{:S(2)}, u32[]{:S(2)}) %collective-permute-start.6) | collective-permute-done | bytes 786464 | tf_op jit(solution)/shard_map/ppermute | solution.py:24
  214.8 7.0 pad_maximum_fusion
  224.6 6.5 pad_maximum_fusion.1
  232.9 15.8 %collective-permute-done.7 = bf16[2,256,1536]{2,1,0:T(8,128)(2,1)} collective-permute-done((bf16[2,256,1536]{2,1,0:T(8,128)(2,1)}, bf16[2,256,1536]{2,1,0:T(8,128)(2,1)}, u32[]{:S(2)}, u32[]{:S(2)}) %collective-permute-start.7) | collective-permute-done | bytes 1572896 | tf_op jit(solution)/shard_map/ppermute | solution.py:24
  252.5 7.8 collective-permute-done.10
  271.1 21.0 %all-gather.23.cloned.1.call-done = bf16[8,192,1536]{2,1,0:T(8,128)(2,1)} async-done(((bf16[2,192,1536]{2,1,0:T(8,128)(2,1)}), bf16[8,192,1536]{2,1,0:T(8,128)(2,1)}) %all-gather.23.cloned.1.call-update) | async-done | bytes 4718608 | tf_op jit(solution)/shard_map/all_gather | solution.py:107
  310.5 70.9 %all-gather.25.cloned.1.call-done = bf16[8,192,1536]{2,1,0:T(8,128)(2,1)} async-done(((bf16[2,192,1536]{2,1,0:T(8,128)(2,1)}), bf16[8,192,1536]{2,1,0:T(8,128)(2,1)}) %all-gather.25.cloned.1.call-update) | async-done | bytes 4718608 | tf_op jit(solution)/shard_map/all_gather | solution.py:107
  425.9 48.6 %copy.55 = bf16[3072,6144]{1,0:T(8,128)(2,1)} copy(bf16[3072,6144]{0,1:T(8,128)(2,1)} %bitcast.28) | data formatting | bytes 75497472 | tf_op jit(solution)/shard_map/dot_general | solution.py:125
  474.5 20.0 %fusion.10 = f32[2,192,3,8,128]{4,1,0,3,2:T(8,128)S(1)} fusion(bf16[3,8,128,6144,1]{3,2,4,1,0:T(8,128)(2,1)} %bitcast.440, bf16[2,192,6144]{2,1,0:T(8,128)(2,1)} %copy-done.37), kind=kOutput, calls=%fused_computation.23 | convolution fusion | flops 14495514624 | bytes 47185920 | tf_op jit(solution)/shard_map/dot_general | solution.py:125
  497.0 20.0 %fusion.4 = f32[2,192,3,8,128]{4,1,0,3,2:T(8,128)S(1)} fusion(bf16[3,8,128,6144,1]{3,2,4,1,0:T(8,128)(2,1)} %bitcast.441, bf16[2,192,6144]{2,1,0:T(8,128)(2,1)} %copy-done.38), kind=kOutput, calls=%fused_computation.17 | convolution fusion | flops 14495514624 | bytes 47185920 | tf_op jit(solution)/shard_map/dot_general | solution.py:125
  519.5 4.9 fusion.29
  546.5 13.2 %all-to-all-done.q_ref.k_ref.v_ref = bf16[8,2,3,192,128]{4,3,2,1,0:T(8,128)(2,1)S(1)} async-done(((bf16[8,2,3,192,128]{4,3,2,1,0:T(8,128)(2,1)}), bf16[8,2,3,192,128]{4,3,2,1,0:T(8,128)(2,1)S(1)}, u32[]{:S(2)}, u32[]{:S(2)}) %all-to-all-start) | async-done | bytes 2359328 | tf_op jit(solution)/shard_map/all_to_all | solution.py:133
  559.7 4.4 all-to-all-start.6
  581.4 16.5 %attend.4 = bf16[8,2,192,128]{3,2,1,0:T(8,128)(2,1)} custom-call(bf16[8,2,3,192,128]{4,3,2,1,0:T(8,128)(2,1)S(1)} %all-to-all-done.q_ref.k_ref.v_ref, bf16[8,2,3,192,128]{4,3,2,1,0:T(8,128)(2,1)S(1)} %all-to-all-done.q_ref.k_ref.v_ref, bf16[8,2,3,192,128]{4,3,2,1,0:T(8,128)(2,1)S(1)} %all-to-all-done.q_ref.k_ref.v_ref), custom_call_target="tpu_custom_call" | custom-call | flops 2415919104 | bytes 3145728 | tf_op jit(solution)/shard_map/attend/pallas_call | solution.py:71
  602.0 21.8 %fusion.8 = f32[2,192,3,8,128]{4,1,0,3,2:T(8,128)} fusion(bf16[3,8,128,6144,1]{3,2,4,1,0:T(8,128)(2,1)} %bitcast.442, bf16[2,192,6144]{2,1,0:T(8,128)(2,1)} %fusion.147), kind=kOutput, calls=%fused_computation.21 | convolution fusion | flops 14495514624 | bytes 47185920 | tf_op jit(solution)/shard_map/dot_general | solution.py:125
  623.8 17.6 %attend.7 = bf16[8,2,192,128]{3,2,1,0:T(8,128)(2,1)} custom-call(bf16[8,2,3,192,128]{4,3,2,1,0:T(8,128)(2,1)} %all-to-all-done.6.q_ref.k_ref.v_ref, bf16[8,2,3,192,128]{4,3,2,1,0:T(8,128)(2,1)} %all-to-all-done.6.q_ref.k_ref.v_ref, bf16[8,2,3,192,128]{4,3,2,1,0:T(8,128)(2,1)} %all-to-all-done.6.q_ref.k_ref.v_ref), custom_call_target="tpu_custom_call" | custom-call | flops 2415919104 | bytes 3145728 | tf_op jit(solution)/shard_map/attend/pallas_call | solution.py:71
  647.5 20.2 %fusion.6 = f32[2,192,3,8,128]{4,1,0,3,2:T(8,128)S(1)} fusion(bf16[3,8,128,6144,1]{3,2,4,1,0:T(8,128)(2,1)} %bitcast.443, bf16[2,192,6144]{2,1,0:T(8,128)(2,1)} %fusion.155), kind=kOutput, calls=%fused_computation.19 | convolution fusion | flops 14495514624 | bytes 47185920 | tf_op jit(solution)/shard_map/dot_general | solution.py:125
  679.7 8.1 fusion.35
  701.4 21.6 %all-to-all-done.2.q_ref.k_ref.v_ref = bf16[8,2,3,192,128]{4,3,2,1,0:T(8,128)(2,1)S(1)} async-done(((bf16[8,2,3,192,128]{4,3,2,1,0:T(8,128)(2,1)}), bf16[8,2,3,192,128]{4,3,2,1,0:T(8,128)(2,1)S(1)}, u32[]{:S(2)}, u32[]{:S(2)}) %all-to-all-start.2) | async-done | bytes 2359328 | tf_op jit(solution)/shard_map/all_to_all | solution.py:133
  723.0 16.5 %attend.5 = bf16[8,2,192,128]{3,2,1,0:T(8,128)(2,1)} custom-call(bf16[8,2,3,192,128]{4,3,2,1,0:T(8,128)(2,1)S(1)} %all-to-all-done.2.q_ref.k_ref.v_ref, bf16[8,2,3,192,128]{4,3,2,1,0:T(8,128)(2,1)S(1)} %all-to-all-done.2.q_ref.k_ref.v_ref, bf16[8,2,3,192,128]{4,3,2,1,0:T(8,128)(2,1)S(1)} %all-to-all-done.2.q_ref.k_ref.v_ref), custom_call_target="tpu_custom_call" | custom-call | flops 2415919104 | bytes 3145728 | tf_op jit(solution)/shard_map/attend/pallas_call | solution.py:71
  747.3 8.3 all-to-all-done.3
  778.0 19.9 %all-to-all-done.4.q_ref.k_ref.v_ref = bf16[8,2,3,192,128]{4,3,2,1,0:T(8,128)(2,1)S(1)} async-done(((bf16[8,2,3,192,128]{4,3,2,1,0:T(8,128)(2,1)}), bf16[8,2,3,192,128]{4,3,2,1,0:T(8,128)(2,1)S(1)}, u32[]{:S(2)}, u32[]{:S(2)}) %all-to-all-start.4) | async-done | bytes 2359328 | tf_op jit(solution)/shard_map/all_to_all | solution.py:133
  797.9 16.5 %attend.6 = bf16[8,2,192,128]{3,2,1,0:T(8,128)(2,1)} custom-call(bf16[8,2,3,192,128]{4,3,2,1,0:T(8,128)(2,1)S(1)} %all-to-all-done.4.q_ref.k_ref.v_ref, bf16[8,2,3,192,128]{4,3,2,1,0:T(8,128)(2,1)S(1)} %all-to-all-done.4.q_ref.k_ref.v_ref, bf16[8,2,3,192,128]{4,3,2,1,0:T(8,128)(2,1)S(1)} %all-to-all-done.4.q_ref.k_ref.v_ref), custom_call_target="tpu_custom_call" | custom-call | flops 2415919104 | bytes 3145728 | tf_op jit(solution)/shard_map/attend/pallas_call | solution.py:71
  822.2 8.3 all-to-all-done.5
  856.8 9.7 %fusion.165 = f32[384,1536]{1,0:T(8,128)} fusion(bf16[384,4096]{1,0:T(8,128)(2,1)S(1)} %copy-done.39, bf16[4096,1536]{1,0:T(8,128)(2,1)} %fusion.120), kind=kOutput, calls=%fused_computation.349 | convolution fusion | flops 4831838208 | bytes 18087936 | tf_op jit(solution)/shard_map/dot_general | solution.py:142
  866.4 11.3 %fusion.168 = f32[384,1536]{1,0:T(8,128)} fusion(bf16[384,4096]{1,0:T(8,128)(2,1)} %bitcast_dynamic-update-slice_fusion.4, bf16[4096,1536]{1,0:T(8,128)(2,1)} %fusion.120), kind=kOutput, calls=%fused_computation.352 | convolution fusion | flops 4831838208 | bytes 18087936 | tf_op jit(solution)/shard_map/dot_general | solution.py:142
  877.8 8.1 fusion.166
  885.8 15.4 %all-gather.17.cloned.1.call-done = bf16[4,384,1024]{2,1,0:T(8,128)(2,1)} async-done(((bf16[1,384,1024]{2,1,0:T(8,128)(2,1)}), bf16[4,384,1024]{2,1,0:T(8,128)(2,1)}) %all-gather.17.cloned.1.call-update) | async-done | bytes 3145744 | tf_op jit(solution)/shard_map/all_gather | solution.py:140
  905.8 8.2 fusion.167
  917.6 4.8 copy.75
  (287 shorter events, 263.1 us)
Async XLA Ops:
  6.5 257.1 %all-gather.21.cloned.1.call-start = ((), (), s32[]{:S(2)}) async-start(), calls=%async_computation.12 | async-start | bytes 5898240 | tf_op jit(solution)/shard_map/all_gather | solution.py:107
  18.7 212.7 %copy-start.8 = (bf16[192,2,1536]{2,1,0:T(2,128)(2,1)}, bf16[192,2,1536]{2,1,0:T(2,128)(2,1)S(1)}, u32[]{:S(2)}) copy-start(bf16[192,2,1536]{2,1,0:T(2,128)(2,1)S(1)} %get-tuple-element.32) | copy-start | bytes 3538948
  20.9 246.5 %all-gather.27.cloned.1.call-start = ((), (), s32[]{:S(2)}) async-start(), calls=%async_computation.15 | async-start | bytes 5898240 | tf_op jit(solution)/shard_map/all_gather | solution.py:107
  22.1 270.0 %all-gather.23.cloned.1.call-start = ((), (), s32[]{:S(2)}) async-start(), calls=%async_computation.13 | async-start | bytes 5898240 | tf_op jit(solution)/shard_map/all_gather | solution.py:107
  30.2 54.2 %collective-permute-start = (bf16[1,384,3072]{2,1,0:T(8,128)(2,1)S(1)}, bf16[1,384,3072]{2,1,0:T(8,128)(2,1)S(1)}, u32[]{:S(2)}, u32[]{:S(2)}) collective-permute-start(bf16[1,384,3072]{2,1,0:T(8,128)(2,1)S(1)} %get-tuple-element.42), channel_id=1, source_target_pairs={{0,8},{4,12},{8,0},{12,4},{16,24},{20,28},{24,16},{28,20},{1,9},{5... | collective-permute-start | bytes 7077896 | tf_op jit(solution)/shard_map/ppermute | solution.py:24
  33.1 57.2 %collective-permute-start.3 = (bf16[1,384,3072]{2,1,0:T(8,128)(2,1)}, bf16[1,384,3072]{2,1,0:T(8,128)(2,1)S(1)}, u32[]{:S(2)}, u32[]{:S(2)}) collective-permute-start(bf16[1,384,3072]{2,1,0:T(8,128)(2,1)} %get-tuple-element.41), channel_id=1, source_target_pairs={{0,16},{4,20},{8,24},{12,28},{16,0},{20,4},{24,8},{28,12},{1,17},{... | collective-permute-start | bytes 7077896 | tf_op jit(solution)/shard_map/ppermute | solution.py:24
  87.3 127.5 %collective-permute-start.1 = (bf16[2,384,3072]{2,1,0:T(8,128)(2,1)}, bf16[2,384,3072]{2,1,0:T(8,128)(2,1)}, u32[]{:S(2)}, u32[]{:S(2)}) collective-permute-start(bf16[2,384,3072]{2,1,0:T(8,128)(2,1)} %pad_maximum_fusion.2), channel_id=1, source_target_pairs={{0,16},{4,20},{8,24},{12,28},{16,0},{20,4},{24,8},{28,12},{1,17},{... | collective-permute-start | bytes 14155784 | tf_op jit(solution)/shard_map/ppermute | solution.py:24
  90.2 291.2 %all-gather.25.cloned.1.call-start = ((), (), s32[]{:S(2)}) async-start(), calls=%async_computation.14 | async-start | bytes 5898240 | tf_op jit(solution)/shard_map/all_gather | solution.py:107
  92.5 122.2 %copy-start.1 = (bf16[1,384,3072]{2,1,0:T(8,128)(2,1)S(1)}, bf16[1,384,3072]{2,1,0:T(8,128)(2,1)}, u32[]{:S(2)}) copy-start(bf16[1,384,3072]{2,1,0:T(8,128)(2,1)} %copy-done) | copy-start | bytes 7077892
  92.5 122.2 %copy-start.4 = (bf16[1,384,3072]{2,1,0:T(8,128)(2,1)S(1)}, bf16[1,384,3072]{2,1,0:T(8,128)(2,1)}, u32[]{:S(2)}) copy-start(bf16[1,384,3072]{2,1,0:T(8,128)(2,1)} %copy-done.3) | copy-start | bytes 7077892
  92.5 132.1 %collective-permute-start.4 = (bf16[2,384,3072]{2,1,0:T(8,128)(2,1)S(1)}, bf16[2,384,3072]{2,1,0:T(8,128)(2,1)S(1)}, u32[]{:S(2)}, u32[]{:S(2)}) collective-permute-start(bf16[2,384,3072]{2,1,0:T(8,128)(2,1)S(1)} %pad_maximum_fusion.3), channel_id=1, source_target_pairs={{0,8},{4,12},{8,0},{12,4},{16,24},{20,28},{24,16},{28,20},{1,9},{5... | collective-permute-start | bytes 14155784 | tf_op jit(solution)/shard_map/ppermute | solution.py:24
  94.2 127.5 %copy-start.23 = (bf16[1,256,1536]{2,1,0:T(8,128)(2,1)}, bf16[1,256,1536]{2,1,0:T(8,128)(2,1)S(1)}, u32[]{:S(2)}) copy-start(bf16[1,256,1536]{2,1,0:T(8,128)(2,1)S(1)} %get-tuple-element.43) | copy-start | bytes 2359300
  94.2 117.7 %collective-permute-start.6 = (bf16[1,256,1536]{2,1,0:T(8,128)(2,1)S(1)}, bf16[1,256,1536]{2,1,0:T(8,128)(2,1)S(1)}, u32[]{:S(2)}, u32[]{:S(2)}) collective-permute-start(bf16[1,256,1536]{2,1,0:T(8,128)(2,1)S(1)} %get-tuple-element.44), channel_id=1, source_target_pairs={{0,8},{4,12},{8,0},{12,4},{16,24},{20,28},{24,16},{28,20},{1,9},{5... | collective-permute-start | bytes 2359304 | tf_op jit(solution)/shard_map/ppermute | solution.py:24
  94.8 126.9 %collective-permute-start.9 = (bf16[1,256,1536]{2,1,0:T(8,128)(2,1)S(1)}, bf16[1,256,1536]{2,1,0:T(8,128)(2,1)S(1)}, u32[]{:S(2)}, u32[]{:S(2)}) collective-permute-start(bf16[1,256,1536]{2,1,0:T(8,128)(2,1)S(1)} %get-tuple-element.43), channel_id=1, source_target_pairs={{0,16},{4,20},{8,24},{12,28},{16,0},{20,4},{24,8},{28,12},{1,17},{... | collective-permute-start | bytes 2359304 | tf_op jit(solution)/shard_map/ppermute | solution.py:24
  214.2 34.5 %collective-permute-start.7 = (bf16[2,256,1536]{2,1,0:T(8,128)(2,1)}, bf16[2,256,1536]{2,1,0:T(8,128)(2,1)}, u32[]{:S(2)}, u32[]{:S(2)}) collective-permute-start(bf16[2,256,1536]{2,1,0:T(8,128)(2,1)} %pad_maximum_fusion.7), channel_id=1, source_target_pairs={{0,16},{4,20},{8,24},{12,28},{16,0},{20,4},{24,8},{28,12},{1,17},{... | collective-permute-start | bytes 4718600 | tf_op jit(solution)/shard_map/ppermute | solution.py:24
  221.7 163.4 %collective-permute-start.2 = (bf16[4,384,3072]{2,1,0:T(8,128)(2,1)}, bf16[4,384,3072]{2,1,0:T(8,128)(2,1)}, u32[]{:S(2)}, u32[]{:S(2)}) collective-permute-start(bf16[4,384,3072]{2,1,0:T(8,128)(2,1)} %pad_maximum_fusion), channel_id=1, source_target_pairs={{0,4},{4,0},{8,12},{12,8},{16,20},{20,16},{24,28},{28,24},{1,5},{5... | collective-permute-start | bytes 28311560 | tf_op jit(solution)/shard_map/ppermute | solution.py:24
  223.1 37.1 %collective-permute-start.10 = (bf16[2,256,1536]{2,1,0:T(8,128)(2,1)}, bf16[2,256,1536]{2,1,0:T(8,128)(2,1)}, u32[]{:S(2)}, u32[]{:S(2)}) collective-permute-start(bf16[2,256,1536]{2,1,0:T(8,128)(2,1)} %pad_maximum_fusion.8), channel_id=1, source_target_pairs={{0,8},{4,12},{8,0},{12,4},{16,24},{20,28},{24,16},{28,20},{1,9},{5... | collective-permute-start | bytes 4718600 | tf_op jit(solution)/shard_map/ppermute | solution.py:24
  231.1 157.2 %collective-permute-start.5 = (bf16[4,384,3072]{2,1,0:T(8,128)(2,1)}, bf16[4,384,3072]{2,1,0:T(8,128)(2,1)}, u32[]{:S(2)}, u32[]{:S(2)}) collective-permute-start(bf16[4,384,3072]{2,1,0:T(8,128)(2,1)} %pad_maximum_fusion.1), channel_id=1, source_target_pairs={{0,4},{4,0},{8,12},{12,8},{16,20},{20,16},{24,28},{28,24},{1,5},{5... | collective-permute-start | bytes 28311560 | tf_op jit(solution)/shard_map/ppermute | solution.py:24
  252.5 443.8 %collective-permute-start.8 = (bf16[4,256,1536]{2,1,0:T(8,128)(2,1)}, bf16[4,256,1536]{2,1,0:T(8,128)(2,1)}, u32[]{:S(2)}, u32[]{:S(2)}) collective-permute-start(bf16[4,256,1536]{2,1,0:T(8,128)(2,1)} %pad_maximum_fusion.5), channel_id=1, source_target_pairs={{0,4},{4,0},{8,12},{12,8},{16,20},{20,16},{24,28},{28,24},{1,5},{5... | collective-permute-start | bytes 9437192 | tf_op jit(solution)/shard_map/ppermute | solution.py:24
  263.6 434.8 %collective-permute-start.11 = (bf16[4,256,1536]{2,1,0:T(8,128)(2,1)}, bf16[4,256,1536]{2,1,0:T(8,128)(2,1)}, u32[]{:S(2)}, u32[]{:S(2)}) collective-permute-start(bf16[4,256,1536]{2,1,0:T(8,128)(2,1)} %pad_maximum_fusion.6), channel_id=1, source_target_pairs={{0,4},{4,0},{8,12},{12,8},{16,20},{20,16},{24,28},{28,24},{1,5},{5... | collective-permute-start | bytes 9437192 | tf_op jit(solution)/shard_map/ppermute | solution.py:24
  526.1 33.6 %all-to-all-start = ((bf16[8,2,3,192,128]{4,3,2,1,0:T(8,128)(2,1)}), bf16[8,2,3,192,128]{4,3,2,1,0:T(8,128)(2,1)S(1)}, u32[]{:S(2)}, u32[]{:S(2)}) async-start(bf16[8,2,3,192,128]{4,3,2,1,0:T(8,128)(2,1)} %maximum_bitcast_fusion), calls=%async_computation | async-start | bytes 4718592 | tf_op jit(solution)/shard_map/all_to_all | solution.py:133
  559.7 38.2 %all-to-all-start.6 = ((bf16[8,2,3,192,128]{4,3,2,1,0:T(8,128)(2,1)}), bf16[8,2,3,192,128]{4,3,2,1,0:T(8,128)(2,1)}, u32[]{:S(2)}, u32[]{:S(2)}) async-start(bf16[8,2,3,192,128]{4,3,2,1,0:T(8,128)(2,1)} %maximum_bitcast_fusion.3), calls=%async_computation.6 | async-start | bytes 4718592 | tf_op jit(solution)/shard_map/all_to_all | solution.py:133
  597.9 43.5 %all-to-all-start.1 = ((bf16[8,2,192,128]{3,2,1,0:T(8,128)(2,1)}), bf16[8,2,192,128]{3,2,1,0:T(8,128)(2,1)S(1)}, u32[]{:S(2)}, u32[]{:S(2)}) async-start(bf16[8,2,192,128]{3,2,1,0:T(8,128)(2,1)} %attend.4), calls=%async_computation.1 | async-start | bytes 1572864 | tf_op jit(solution)/shard_map/all_to_all | solution.py:134
  641.4 34.9 %all-to-all-start.7 = ((bf16[8,2,192,128]{3,2,1,0:T(8,128)(2,1)}), bf16[8,2,192,128]{3,2,1,0:T(8,128)(2,1)S(1)}, u32[]{:S(2)}, u32[]{:S(2)}) async-start(bf16[8,2,192,128]{3,2,1,0:T(8,128)(2,1)} %attend.7), calls=%async_computation.7 | async-start | bytes 1572864 | tf_op jit(solution)/shard_map/all_to_all | solution.py:134
  645.6 186.8 %all-gather.13.cloned.1.call-start = ((), (), s32[]{:S(2)}) async-start(), calls=%async_computation.8 | async-start | bytes 3932160 | tf_op jit(solution)/shard_map/all_gather | solution.py:140
  647.4 186.9 %all-gather.19.cloned.1.call-start = ((), (), s32[]{:S(2)}) async-start(), calls=%async_computation.11 | async-start | bytes 3932160 | tf_op jit(solution)/shard_map/all_gather | solution.py:140
  689.4 33.6 %all-to-all-start.2 = ((bf16[8,2,3,192,128]{4,3,2,1,0:T(8,128)(2,1)}), bf16[8,2,3,192,128]{4,3,2,1,0:T(8,128)(2,1)S(1)}, u32[]{:S(2)}, u32[]{:S(2)}) async-start(bf16[8,2,3,192,128]{4,3,2,1,0:T(8,128)(2,1)} %maximum_bitcast_fusion.1), calls=%async_computation.2 | async-start | bytes 4718592 | tf_op jit(solution)/shard_map/all_to_all | solution.py:133
  739.5 16.1 %all-to-all-start.3 = ((bf16[8,2,192,128]{3,2,1,0:T(8,128)(2,1)}), bf16[8,2,192,128]{3,2,1,0:T(8,128)(2,1)S(1)}, u32[]{:S(2)}, u32[]{:S(2)}) async-start(bf16[8,2,192,128]{3,2,1,0:T(8,128)(2,1)} %attend.5), calls=%async_computation.3 | async-start | bytes 1572864 | tf_op jit(solution)/shard_map/all_to_all | solution.py:134
  743.0 108.5 %all-gather.15.cloned.1.call-start = ((), (), s32[]{:S(2)}) async-start(), calls=%async_computation.9 | async-start | bytes 3932160 | tf_op jit(solution)/shard_map/all_gather | solution.py:140
  764.8 33.1 %all-to-all-start.4 = ((bf16[8,2,3,192,128]{4,3,2,1,0:T(8,128)(2,1)}), bf16[8,2,3,192,128]{4,3,2,1,0:T(8,128)(2,1)S(1)}, u32[]{:S(2)}, u32[]{:S(2)}) async-start(bf16[8,2,3,192,128]{4,3,2,1,0:T(8,128)(2,1)} %maximum_bitcast_fusion.2), calls=%async_computation.4 | async-start | bytes 4718592 | tf_op jit(solution)/shard_map/all_to_all | solution.py:133
  814.4 16.1 %all-to-all-start.5 = ((bf16[8,2,192,128]{3,2,1,0:T(8,128)(2,1)}), bf16[8,2,192,128]{3,2,1,0:T(8,128)(2,1)S(1)}, u32[]{:S(2)}, u32[]{:S(2)}) async-start(bf16[8,2,192,128]{3,2,1,0:T(8,128)(2,1)} %attend.6), calls=%async_computation.5 | async-start | bytes 1572864 | tf_op jit(solution)/shard_map/all_to_all | solution.py:134
  818.0 83.3 %all-gather.17.cloned.1.call-start = ((), (), s32[]{:S(2)}) async-start(), calls=%async_computation.10 | async-start | bytes 3932160 | tf_op jit(solution)/shard_map/all_gather | solution.py:140
  (40 other events, 463.1 us)
Sparse Core Ops, SparseCore 0:
  21.0 92.0 all-gather.20
  114.7 87.8 all-gather.26
  204.2 87.8 all-gather.22
  293.5 87.8 all-gather.24
  647.7 62.4 all-gather.12
  711.6 62.1 all-gather.18
  775.3 62.1 all-gather.14
  839.1 62.1 all-gather.16

commit v2 on v1

--- a/solution.py
+++ b/solution.py
@@ -106,11 +106,14 @@
         ]
         wholes = [lax.all_gather(m, "wid", axis=0, tiled=False) for m in mine]
         w_in = gather_rows(jnp.concatenate([w_query, w_key, w_value], axis=1), "tok", toks)
+        w_in, w_out = lax.optimization_barrier((w_in, w_out))
         w_last = gather_rows(w_out, "tok", toks)
 
-        outs = []
+        projected = []
         for g in range(groups):
             whole = wholes[g]
+            if g == groups - 1 and g > 0:
+                whole, projected[g - 1] = lax.optimization_barrier((whole, projected[g - 1]))
             as_float = whole.astype(jnp.float32)
             mean = jnp.sum(as_float, axis=(0, 3)) / model
             var = jnp.sum(as_float * as_float, axis=(0, 3)) / model - mean * mean
@@ -122,8 +125,12 @@
                 ],
                 axis=-1,
             ).reshape(group * rows, model)
-            qkv = jnp.dot(normed, w_in, preferred_element_type=jnp.float32)
-            qkv = qkv.reshape(group, rows, 3, heads, HEAD_DIM)
+            product = jnp.dot(normed, w_in, preferred_element_type=jnp.float32)
+            projected.append(lax.optimization_barrier(product))
+
+        outs = []
+        for g in range(groups):
+            qkv = projected[g].reshape(group, rows, 3, heads, HEAD_DIM)
             qn = (layer_norm_rows(qkv[:, :, 0], EPS) * q_gain.reshape(heads, HEAD_DIM)).astype(jnp.bfloat16)
             kn = (layer_norm_rows(qkv[:, :, 1], EPS) * k_gain.reshape(heads, HEAD_DIM)).astype(jnp.bfloat16)
             vb = qkv[:, :, 2].astype(jnp.bfloat16)

time: 939 us -> 902 us (0.961)
  blocking collectives: 0 us -> 95.1 us
  waiting for transfers between devices: 369 us -> 318 us
  other arithmetic: 118 us -> 87 us
  local copies, waits for them, and re-layouts: 198 us -> 172 us
  starting transfers between devices: 43 us -> 29.4 us
    all_to_all x0 -> x4, blocking collectives: none -> 95.1 us  [the longest x2 65.2 us: local(): lax.all_to_all(packed, 'tok', split_axis=0, concat_axis=0, tiled=False)]
    dot_general x1 -> x0, local copies, waits for them, and re-layouts: 48.6 us -> none  [local(): qkv = jnp.dot(normed, w_in, preferred_element_type=jnp.float32)]
    unnamed x29 -> x34, other arithmetic: 35.7 us -> 9.45 us
    ppermute x12, waiting for transfers between devices: 190 us -> 169 us  [xor_gather(): got = lax.ppermute(data, axis, [(i, i ^ step) for i in range(count)])]
    all_gather x4, waiting for transfers between devices: 15.4 us -> 0.03 us  [local(): every = lax.all_gather(mixed, 'wid', axis=0, tiled=False)]
    all_gather x4, waiting for transfers between devices: 91.9 us -> 82.3 us  [local(): wholes = [lax.all_gather(m, 'wid', axis=0, tiled=False) for m in mine]]
    unnamed x149 -> x179, local copies, waits for them, and re-layouts: 111 us -> 119 us
    all_to_all x4 -> x2, waiting for transfers between devices: 54.7 us -> 49.1 us  [local(): lax.all_to_all(packed, 'tok', split_axis=0, concat_axis=0, tiled=False)]
  transfers between devices with their start and end apart: 28 -> 24, of which waited for: 12 -> 9; matrix products, arithmetic and copies ran while one was open for 42% -> 25% of each run, Pallas kernels for 7% -> 5%
where the time goes in v2:
time: 902 us; the launch traced here: 894 us
  waiting for transfers between devices  318 us (35%)
  local copies, waits for them, and re-layouts  172 us (19%)
  matrix products  112 us (12%)
  blocking collectives  95.1 us (11%)
  other arithmetic  87 us (10%)
  Pallas kernels  64.9 us (7%)
  starting transfers between devices  29.4 us (3%)
  between operations  15.5 us (2%)
    ppermute x12, waiting for transfers between devices, xor_gather(): got = lax.ppermute(data, axis, [(i, i ^ step) for i in range(count)])  169 us
    unnamed x179, local copies, waits for them, and re-layouts  119 us
    all_gather x4, waiting for transfers between devices, local(): wholes = [lax.all_gather(m, 'wid', axis=0, tiled=False) for m in mine]  82.3 us
    dot_general x4, matrix products, local(): product = jnp.dot(normed, w_in, preferred_element_type=jnp.float32)  80.3 us
    all_to_all x2, blocking collectives, local(): lax.all_to_all(packed, 'tok', split_axis=0, concat_axis=0, tiled=False)  65.2 us
    pallas_call x4, Pallas kernels, attend(): pl.pallas_call(attend_kernel, grid=(items, toks // step), in_specs=[pl.Bl...  64.9 us
    all_to_all x2, waiting for transfers between devices, local(): lax.all_to_all(packed, 'tok', split_axis=0, concat_axis=0, tiled=False)  49.1 us
    concatenate x8, other arithmetic, xor_gather(): data = jnp.concatenate([data, got], axis=0)  34.9 us
  transfers between devices with their start and end apart: 24, of which 9 were waited for; matrix products, arithmetic and copies ran while one was open for 25% of the time, Pallas kernels for 5%

profile of v2, /device:TPU:0, one launch (start us, length us, event | category | flops | bytes accessed | tf_op | source)
XLA Modules:
  0.0 894.2 jit_solution(2073653506616475011)
XLA Ops:
  6.5 12.1 %fusion.157 = (bf16[192,2,1536]{2,1,0:T(2,128)(2,1)}, bf16[192,2,1536]{2,1,0:T(2,128)(2,1)S(1)}, bf16[192,2,1536]{2,1,0:T(2,128)(2,1)S(1)}, bf16[192,2,1536]{2,1,0:T(2,128)(2,1)S(1)}) fusion(bf16[192,8,1536]{2,1,0:T(8,128)(2,1)} %param.7), kind=kLoop, calls=%fused_computation.377 | loop fusion | bytes 9437184 | tf_op jit(solution)/shard_map/slice | solution.py:105
  36.9 48.6 %collective-permute-done = bf16[1,384,3072]{2,1,0:T(8,128)(2,1)S(1)} collective-permute-done((bf16[1,384,3072]{2,1,0:T(8,128)(2,1)}, bf16[1,384,3072]{2,1,0:T(8,128)(2,1)S(1)}, u32[]{:S(2)}, u32[]{:S(2)}) %collective-permute-start) | collective-permute-done | bytes 2359328 | tf_op jit(solution)/shard_map/ppermute | solution.py:24
  97.5 95.8 %collective-permute-done.1 = bf16[2,384,3072]{2,1,0:T(8,128)(2,1)} collective-permute-done((bf16[2,384,3072]{2,1,0:T(8,128)(2,1)}, bf16[2,384,3072]{2,1,0:T(8,128)(2,1)}, u32[]{:S(2)}, u32[]{:S(2)}) %collective-permute-start.1) | collective-permute-done | bytes 4718624 | tf_op jit(solution)/shard_map/ppermute | solution.py:24
  193.2 8.1 pad_maximum_fusion
  205.2 7.2 pad_maximum_fusion.1
  217.1 74.9 %all-gather.21.cloned.1.call-done = bf16[8,192,1536]{2,1,0:T(8,128)(2,1)} async-done(((bf16[2,192,1536]{2,1,0:T(8,128)(2,1)}), bf16[8,192,1536]{2,1,0:T(8,128)(2,1)}) %all-gather.21.cloned.1.call-update) | async-done | bytes 4718608 | tf_op jit(solution)/shard_map/all_gather | solution.py:107
  308.6 4.9 fusion.15
  352.6 21.4 %fusion.165 = f32[384,3072]{1,0:T(8,128)} fusion(bf16[384,6144]{1,0:T(8,128)(2,1)S(1)} %fusion.147, bf16[6144,3072]{1,0:T(8,128)(2,1)} %fusion.4), kind=kOutput, calls=%fused_computation.385 | convolution fusion | flops 14495514624 | bytes 47185920 | tf_op jit(solution)/shard_map/dot_general | solution.py:128
  374.0 7.3 all-gather.25.cloned.1.call-done
  387.5 19.4 %fusion.163 = f32[384,3072]{1,0:T(8,128)S(1)} fusion(bf16[384,6144]{1,0:T(8,128)(2,1)S(1)} %bitcast.479, bf16[6144,3072]{1,0:T(8,128)(2,1)} %fusion.4), kind=kOutput, calls=%fused_computation.383 | convolution fusion | flops 14495514624 | bytes 47185920 | tf_op jit(solution)/shard_map/dot_general | solution.py:128
  414.6 19.8 %fusion.167 = f32[384,3072]{1,0:T(8,128)S(1)} fusion(bf16[384,6144]{1,0:T(8,128)(2,1)S(1)} %fusion.155, bf16[6144,3072]{1,0:T(8,128)(2,1)} %fusion.4), kind=kOutput, calls=%fused_computation.387 | convolution fusion | flops 14495514624 | bytes 47185920 | tf_op jit(solution)/shard_map/dot_general | solution.py:128
  444.4 19.6 %fusion.161 = f32[384,3072]{1,0:T(8,128)S(1)} fusion(bf16[384,6144]{1,0:T(8,128)(2,1)S(1)} %bitcast.481, bf16[6144,3072]{1,0:T(8,128)(2,1)} %fusion.4), kind=kOutput, calls=%fused_computation.381 | convolution fusion | flops 14495514624 | bytes 47185920 | tf_op jit(solution)/shard_map/dot_general | solution.py:128
  473.6 5.3 fusion.39
  478.9 4.9 fusion.36
  484.0 33.3 %all_to_all.40.q_ref.k_ref.v_ref = bf16[8,2,3,192,128]{4,3,2,1,0:T(8,128)(2,1)S(1)} all-to-all(bf16[8,2,3,192,128]{4,3,2,1,0:T(8,128)(2,1)S(1)} %maximum_bitcast_fusion.1), channel_id=1, replica_groups=mesh['tok'=8,'wid'=4] {'tok'}, dimensions={0} | all-to-all | bytes 4718592 | tf_op jit(solution)/shard_map/all_to_all | solution.py:140
  517.3 15.9 %attend.5 = bf16[8,2,192,128]{3,2,1,0:T(8,128)(2,1)S(1)} custom-call(bf16[8,2,3,192,128]{4,3,2,1,0:T(8,128)(2,1)S(1)} %all_to_all.40.q_ref.k_ref.v_ref, bf16[8,2,3,192,128]{4,3,2,1,0:T(8,128)(2,1)S(1)} %all_to_all.40.q_ref.k_ref.v_ref, bf16[8,2,3,192,128]{4,3,2,1,0:T(8,128)(2,1)S(1)} %all_to_all.40.q_ref.k_ref.v_ref), custom_call_target="tpu_custom_call" | custom-call | flops 2415919104 | bytes 3145728 | tf_op jit(solution)/shard_map/attend/pallas_call | solution.py:71
  533.3 15.0 %all_to_all.41 = bf16[8,2,192,128]{3,2,1,0:T(8,128)(2,1)S(1)} all-to-all(bf16[8,2,192,128]{3,2,1,0:T(8,128)(2,1)S(1)} %attend.5), channel_id=1, replica_groups=mesh['tok'=8,'wid'=4] {'tok'}, dimensions={0} | all-to-all | bytes 1572864 | tf_op jit(solution)/shard_map/all_to_all | solution.py:141
  552.0 31.9 %all_to_all.42.q_ref.k_ref.v_ref = bf16[8,2,3,192,128]{4,3,2,1,0:T(8,128)(2,1)S(1)} all-to-all(bf16[8,2,3,192,128]{4,3,2,1,0:T(8,128)(2,1)S(1)} %maximum_bitcast_fusion), channel_id=1, replica_groups=mesh['tok'=8,'wid'=4] {'tok'}, dimensions={0} | all-to-all | bytes 4718592 | tf_op jit(solution)/shard_map/all_to_all | solution.py:140
  583.8 15.9 %attend.4 = bf16[8,2,192,128]{3,2,1,0:T(8,128)(2,1)S(1)} custom-call(bf16[8,2,3,192,128]{4,3,2,1,0:T(8,128)(2,1)S(1)} %all_to_all.42.q_ref.k_ref.v_ref, bf16[8,2,3,192,128]{4,3,2,1,0:T(8,128)(2,1)S(1)} %all_to_all.42.q_ref.k_ref.v_ref, bf16[8,2,3,192,128]{4,3,2,1,0:T(8,128)(2,1)S(1)} %all_to_all.42.q_ref.k_ref.v_ref), custom_call_target="tpu_custom_call" | custom-call | flops 2415919104 | bytes 3145728 | tf_op jit(solution)/shard_map/attend/pallas_call | solution.py:71
  599.8 15.0 %all_to_all.43 = bf16[8,2,192,128]{3,2,1,0:T(8,128)(2,1)S(1)} all-to-all(bf16[8,2,192,128]{3,2,1,0:T(8,128)(2,1)S(1)} %attend.4), channel_id=1, replica_groups=mesh['tok'=8,'wid'=4] {'tok'}, dimensions={0} | all-to-all | bytes 1572864 | tf_op jit(solution)/shard_map/all_to_all | solution.py:141
  629.6 23.8 %all-to-all-done.6.q_ref.k_ref.v_ref = bf16[8,2,3,192,128]{4,3,2,1,0:T(8,128)(2,1)S(1)} async-done(((bf16[8,2,3,192,128]{4,3,2,1,0:T(8,128)(2,1)}), bf16[8,2,3,192,128]{4,3,2,1,0:T(8,128)(2,1)S(1)}, u32[]{:S(2)}, u32[]{:S(2)}) %all-to-all-start.6) | async-done | bytes 2359328 | tf_op jit(solution)/shard_map/all_to_all | solution.py:140
  653.4 16.5 %attend.7 = bf16[8,2,192,128]{3,2,1,0:T(8,128)(2,1)} custom-call(bf16[8,2,3,192,128]{4,3,2,1,0:T(8,128)(2,1)S(1)} %all-to-all-done.6.q_ref.k_ref.v_ref, bf16[8,2,3,192,128]{4,3,2,1,0:T(8,128)(2,1)S(1)} %all-to-all-done.6.q_ref.k_ref.v_ref, bf16[8,2,3,192,128]{4,3,2,1,0:T(8,128)(2,1)S(1)} %all-to-all-done.6.q_ref.k_ref.v_ref), custom_call_target="tpu_custom_call" | custom-call | flops 2415919104 | bytes 3145728 | tf_op jit(solution)/shard_map/attend/pallas_call | solution.py:71
  678.0 8.0 all-to-all-done.7
  694.4 24.3 %collective-permute-done.7 = bf16[2,256,1536]{2,1,0:T(8,128)(2,1)S(1)} collective-permute-done((bf16[2,256,1536]{2,1,0:T(8,128)(2,1)}, bf16[2,256,1536]{2,1,0:T(8,128)(2,1)S(1)}, u32[]{:S(2)}, u32[]{:S(2)}) %collective-permute-start.7) | collective-permute-done | bytes 1572896 | tf_op jit(solution)/shard_map/ppermute | solution.py:24
  732.2 25.4 %all-to-all-done.4.q_ref.k_ref.v_ref = bf16[8,2,3,192,128]{4,3,2,1,0:T(8,128)(2,1)S(1)} async-done(((bf16[8,2,3,192,128]{4,3,2,1,0:T(8,128)(2,1)}), bf16[8,2,3,192,128]{4,3,2,1,0:T(8,128)(2,1)S(1)}, u32[]{:S(2)}, u32[]{:S(2)}) %all-to-all-start.4) | async-done | bytes 2359328 | tf_op jit(solution)/shard_map/all_to_all | solution.py:140
  757.5 16.5 %attend.6 = bf16[8,2,192,128]{3,2,1,0:T(8,128)(2,1)} custom-call(bf16[8,2,3,192,128]{4,3,2,1,0:T(8,128)(2,1)S(1)} %all-to-all-done.4.q_ref.k_ref.v_ref, bf16[8,2,3,192,128]{4,3,2,1,0:T(8,128)(2,1)S(1)} %all-to-all-done.4.q_ref.k_ref.v_ref, bf16[8,2,3,192,128]{4,3,2,1,0:T(8,128)(2,1)S(1)} %all-to-all-done.4.q_ref.k_ref.v_ref), custom_call_target="tpu_custom_call" | custom-call | flops 2415919104 | bytes 3145728 | tf_op jit(solution)/shard_map/attend/pallas_call | solution.py:71
  780.4 9.7 %all-to-all-done.5 = bf16[8,2,192,128]{3,2,1,0:T(8,128)(2,1)S(1)} async-done(((bf16[8,2,192,128]{3,2,1,0:T(8,128)(2,1)}), bf16[8,2,192,128]{3,2,1,0:T(8,128)(2,1)S(1)}, u32[]{:S(2)}, u32[]{:S(2)}) %all-to-all-start.5) | async-done | bytes 786464 | tf_op jit(solution)/shard_map/all_to_all | solution.py:141
  842.1 11.0 %fusion.164 = f32[384,1536]{1,0:T(8,128)} fusion(bf16[384,4096]{1,0:T(8,128)(2,1)S(1)} %copy-done.39, bf16[4096,1536]{1,0:T(8,128)(2,1)} %fusion.112), kind=kOutput, calls=%fused_computation.384 | convolution fusion | flops 4831838208 | bytes 18087936 | tf_op jit(solution)/shard_map/dot_general | solution.py:149
  853.1 7.8 fusion.162
  860.9 5.1 fusion.168
  870.6 8.2 fusion.166
  882.3 4.8 copy.67
  (345 shorter events, 241.2 us)
Async XLA Ops:
  6.5 194.8 %all-gather.27.cloned.1.call-start = ((), (), s32[]{:S(2)}) async-start(), calls=%async_computation.15 | async-start | bytes 5898240 | tf_op jit(solution)/shard_map/all_gather | solution.py:107
  18.7 77.2 %copy-start.11 = (bf16[192,2,1536]{2,1,0:T(2,128)(2,1)}, bf16[192,2,1536]{2,1,0:T(2,128)(2,1)S(1)}, u32[]{:S(2)}) copy-start(bf16[192,2,1536]{2,1,0:T(2,128)(2,1)S(1)} %get-tuple-element.50) | copy-start | bytes 3538948
  20.9 192.2 %all-gather.23.cloned.1.call-start = ((), (), s32[]{:S(2)}) async-start(), calls=%async_computation.13 | async-start | bytes 5898240 | tf_op jit(solution)/shard_map/all_gather | solution.py:107
  22.1 270.0 %all-gather.21.cloned.1.call-start = ((), (), s32[]{:S(2)}) async-start(), calls=%async_computation.12 | async-start | bytes 5898240 | tf_op jit(solution)/shard_map/all_gather | solution.py:107
  31.1 54.4 %collective-permute-start = (bf16[1,384,3072]{2,1,0:T(8,128)(2,1)}, bf16[1,384,3072]{2,1,0:T(8,128)(2,1)S(1)}, u32[]{:S(2)}, u32[]{:S(2)}) collective-permute-start(bf16[1,384,3072]{2,1,0:T(8,128)(2,1)} %get-tuple-element.74), channel_id=1, source_target_pairs={{0,8},{4,12},{8,0},{12,4},{16,24},{20,28},{24,16},{28,20},{1,9},{5... | collective-permute-start | bytes 7077896 | tf_op jit(solution)/shard_map/ppermute | solution.py:24
  35.3 346.1 %all-gather.25.cloned.1.call-start = ((), (), s32[]{:S(2)}) async-start(), calls=%async_computation.14 | async-start | bytes 5898240 | tf_op jit(solution)/shard_map/all_gather | solution.py:107
  35.3 56.3 %copy-start.3 = (bf16[1,384,3072]{2,1,0:T(8,128)(2,1)S(1)}, bf16[1,384,3072]{2,1,0:T(8,128)(2,1)}, u32[]{:S(2)}) copy-start(bf16[1,384,3072]{2,1,0:T(8,128)(2,1)} %get-tuple-element.73) | copy-start | bytes 7077892
  35.3 56.3 %collective-permute-start.3 = (bf16[1,384,3072]{2,1,0:T(8,128)(2,1)}, bf16[1,384,3072]{2,1,0:T(8,128)(2,1)S(1)}, u32[]{:S(2)}, u32[]{:S(2)}) collective-permute-start(bf16[1,384,3072]{2,1,0:T(8,128)(2,1)} %get-tuple-element.73), channel_id=1, source_target_pairs={{0,16},{4,20},{8,24},{12,28},{16,0},{20,4},{24,8},{28,12},{1,17},{... | collective-permute-start | bytes 7077896 | tf_op jit(solution)/shard_map/ppermute | solution.py:24
  89.8 103.4 %collective-permute-start.1 = (bf16[2,384,3072]{2,1,0:T(8,128)(2,1)}, bf16[2,384,3072]{2,1,0:T(8,128)(2,1)}, u32[]{:S(2)}, u32[]{:S(2)}) collective-permute-start(bf16[2,384,3072]{2,1,0:T(8,128)(2,1)} %pad_maximum_fusion.2), channel_id=1, source_target_pairs={{0,16},{4,20},{8,24},{12,28},{16,0},{20,4},{24,8},{28,12},{1,17},{... | collective-permute-start | bytes 14155784 | tf_op jit(solution)/shard_map/ppermute | solution.py:24
  94.4 110.8 %collective-permute-start.4 = (bf16[2,384,3072]{2,1,0:T(8,128)(2,1)}, bf16[2,384,3072]{2,1,0:T(8,128)(2,1)}, u32[]{:S(2)}, u32[]{:S(2)}) collective-permute-start(bf16[2,384,3072]{2,1,0:T(8,128)(2,1)} %pad_maximum_fusion.3), channel_id=1, source_target_pairs={{0,8},{4,12},{8,0},{12,4},{16,24},{20,28},{24,16},{28,20},{1,9},{5... | collective-permute-start | bytes 14155784 | tf_op jit(solution)/shard_map/ppermute | solution.py:24
  97.1 720.9 %all-gather.15.cloned.1.call-start = ((), (), s32[]{:S(2)}) async-start(), calls=%async_computation.9 | async-start | bytes 3932160 | tf_op jit(solution)/shard_map/all_gather | solution.py:147
  201.3 107.3 %collective-permute-start.2 = (bf16[4,384,3072]{2,1,0:T(8,128)(2,1)}, bf16[4,384,3072]{2,1,0:T(8,128)(2,1)}, u32[]{:S(2)}, u32[]{:S(2)}) collective-permute-start(bf16[4,384,3072]{2,1,0:T(8,128)(2,1)} %pad_maximum_fusion), channel_id=1, source_target_pairs={{0,4},{4,0},{8,12},{12,8},{16,20},{20,16},{24,28},{28,24},{1,5},{5... | collective-permute-start | bytes 28311560 | tf_op jit(solution)/shard_map/ppermute | solution.py:24
  212.5 101.1 %collective-permute-start.5 = (bf16[4,384,3072]{2,1,0:T(8,128)(2,1)}, bf16[4,384,3072]{2,1,0:T(8,128)(2,1)}, u32[]{:S(2)}, u32[]{:S(2)}) collective-permute-start(bf16[4,384,3072]{2,1,0:T(8,128)(2,1)} %pad_maximum_fusion.1), channel_id=1, source_target_pairs={{0,4},{4,0},{8,12},{12,8},{16,20},{20,16},{24,28},{28,24},{1,5},{5... | collective-permute-start | bytes 28311560 | tf_op jit(solution)/shard_map/ppermute | solution.py:24
  550.0 269.9 %all-gather.13.cloned.1.call-start = ((), (), s32[]{:S(2)}) async-start(), calls=%async_computation.8 | async-start | bytes 3932160 | tf_op jit(solution)/shard_map/all_gather | solution.py:147
  619.8 33.6 %all-to-all-start.6 = ((bf16[8,2,3,192,128]{4,3,2,1,0:T(8,128)(2,1)}), bf16[8,2,3,192,128]{4,3,2,1,0:T(8,128)(2,1)S(1)}, u32[]{:S(2)}, u32[]{:S(2)}) async-start(bf16[8,2,3,192,128]{4,3,2,1,0:T(8,128)(2,1)} %maximum_bitcast_fusion.3), calls=%async_computation.6 | async-start | bytes 4718592 | tf_op jit(solution)/shard_map/all_to_all | solution.py:140
  626.2 47.3 %collective-permute-start.6 = (bf16[1,256,1536]{2,1,0:T(8,128)(2,1)}, bf16[1,256,1536]{2,1,0:T(8,128)(2,1)}, u32[]{:S(2)}, u32[]{:S(2)}) collective-permute-start(bf16[1,256,1536]{2,1,0:T(8,128)(2,1)} %get-tuple-element.84), channel_id=1, source_target_pairs={{0,8},{4,12},{8,0},{12,4},{16,24},{20,28},{24,16},{28,20},{1,9},{5... | collective-permute-start | bytes 2359304 | tf_op jit(solution)/shard_map/ppermute | solution.py:24
  628.1 61.6 %collective-permute-start.9 = (bf16[1,256,1536]{2,1,0:T(8,128)(2,1)}, bf16[1,256,1536]{2,1,0:T(8,128)(2,1)S(1)}, u32[]{:S(2)}, u32[]{:S(2)}) collective-permute-start(bf16[1,256,1536]{2,1,0:T(8,128)(2,1)} %get-tuple-element.83), channel_id=1, source_target_pairs={{0,16},{4,20},{8,24},{12,28},{16,0},{20,4},{24,8},{28,12},{1,17},{... | collective-permute-start | bytes 2359304 | tf_op jit(solution)/shard_map/ppermute | solution.py:24
  669.9 16.2 %all-to-all-start.7 = ((bf16[8,2,192,128]{3,2,1,0:T(8,128)(2,1)}), bf16[8,2,192,128]{3,2,1,0:T(8,128)(2,1)S(1)}, u32[]{:S(2)}, u32[]{:S(2)}) async-start(bf16[8,2,192,128]{3,2,1,0:T(8,128)(2,1)} %attend.7), calls=%async_computation.7 | async-start | bytes 1572864 | tf_op jit(solution)/shard_map/all_to_all | solution.py:141
  673.4 163.5 %all-gather.19.cloned.1.call-start = ((), (), s32[]{:S(2)}) async-start(), calls=%async_computation.11 | async-start | bytes 3932160 | tf_op jit(solution)/shard_map/all_gather | solution.py:147
  676.1 42.6 %collective-permute-start.7 = (bf16[2,256,1536]{2,1,0:T(8,128)(2,1)}, bf16[2,256,1536]{2,1,0:T(8,128)(2,1)S(1)}, u32[]{:S(2)}, u32[]{:S(2)}) collective-permute-start(bf16[2,256,1536]{2,1,0:T(8,128)(2,1)} %pad_maximum_fusion.7), channel_id=1, source_target_pairs={{0,16},{4,20},{8,24},{12,28},{16,0},{20,4},{24,8},{28,12},{1,17},{... | collective-permute-start | bytes 4718600 | tf_op jit(solution)/shard_map/ppermute | solution.py:24
  692.1 36.0 %collective-permute-start.10 = (bf16[2,256,1536]{2,1,0:T(8,128)(2,1)}, bf16[2,256,1536]{2,1,0:T(8,128)(2,1)}, u32[]{:S(2)}, u32[]{:S(2)}) collective-permute-start(bf16[2,256,1536]{2,1,0:T(8,128)(2,1)} %pad_maximum_fusion.8), channel_id=1, source_target_pairs={{0,8},{4,12},{8,0},{12,4},{16,24},{20,28},{24,16},{28,20},{1,9},{5... | collective-permute-start | bytes 4718600 | tf_op jit(solution)/shard_map/ppermute | solution.py:24
  694.4 28.3 %copy-start.19 = (bf16[1,2,192,8,128]{4,2,0,1,3:T(8,128)(2,1)S(1)}, bf16[1,2,192,8,128]{4,2,0,1,3:T(8,128)(2,1)}, u32[]{:S(2)}) copy-start(bf16[1,2,192,8,128]{4,2,0,1,3:T(8,128)(2,1)} %get-tuple-element.109) | copy-start | bytes 2359300
  694.4 28.2 %copy-start.20 = (bf16[1,2,192,8,128]{4,2,0,1,3:T(8,128)(2,1)S(1)}, bf16[1,2,192,8,128]{4,2,0,1,3:T(8,128)(2,1)}, u32[]{:S(2)}) copy-start(bf16[1,2,192,8,128]{4,2,0,1,3:T(8,128)(2,1)} %get-tuple-element.113) | copy-start | bytes 2359300
  722.6 69.3 %collective-permute-start.8 = (bf16[4,256,1536]{2,1,0:T(8,128)(2,1)}, bf16[4,256,1536]{2,1,0:T(8,128)(2,1)}, u32[]{:S(2)}, u32[]{:S(2)}) collective-permute-start(bf16[4,256,1536]{2,1,0:T(8,128)(2,1)} %pad_maximum_fusion.5), channel_id=1, source_target_pairs={{0,4},{4,0},{8,12},{12,8},{16,20},{20,16},{24,28},{28,24},{1,5},{5... | collective-permute-start | bytes 9437192 | tf_op jit(solution)/shard_map/ppermute | solution.py:24
  724.4 33.2 %all-to-all-start.4 = ((bf16[8,2,3,192,128]{4,3,2,1,0:T(8,128)(2,1)}), bf16[8,2,3,192,128]{4,3,2,1,0:T(8,128)(2,1)S(1)}, u32[]{:S(2)}, u32[]{:S(2)}) async-start(bf16[8,2,3,192,128]{4,3,2,1,0:T(8,128)(2,1)} %maximum_bitcast_fusion.2), calls=%async_computation.4 | async-start | bytes 4718592 | tf_op jit(solution)/shard_map/all_to_all | solution.py:140
  731.7 62.3 %collective-permute-start.11 = (bf16[4,256,1536]{2,1,0:T(8,128)(2,1)}, bf16[4,256,1536]{2,1,0:T(8,128)(2,1)}, u32[]{:S(2)}, u32[]{:S(2)}) collective-permute-start(bf16[4,256,1536]{2,1,0:T(8,128)(2,1)} %pad_maximum_fusion.6), channel_id=1, source_target_pairs={{0,4},{4,0},{8,12},{12,8},{16,20},{20,16},{24,28},{28,24},{1,5},{5... | collective-permute-start | bytes 9437192 | tf_op jit(solution)/shard_map/ppermute | solution.py:24
  774.0 16.1 %all-to-all-start.5 = ((bf16[8,2,192,128]{3,2,1,0:T(8,128)(2,1)}), bf16[8,2,192,128]{3,2,1,0:T(8,128)(2,1)S(1)}, u32[]{:S(2)}, u32[]{:S(2)}) async-start(bf16[8,2,192,128]{3,2,1,0:T(8,128)(2,1)} %attend.6), calls=%async_computation.5 | async-start | bytes 1572864 | tf_op jit(solution)/shard_map/all_to_all | solution.py:141
  777.6 88.5 %all-gather.17.cloned.1.call-start = ((), (), s32[]{:S(2)}) async-start(), calls=%async_computation.10 | async-start | bytes 3932160 | tf_op jit(solution)/shard_map/all_gather | solution.py:147
  819.9 11.5 %copy-start.24 = (bf16[4,384,1024]{2,1,0:T(8,128)(2,1)S(1)}, bf16[4,384,1024]{2,1,0:T(8,128)(2,1)}, u32[]{:S(2)}) copy-start(bf16[4,384,1024]{2,1,0:T(8,128)(2,1)} %all-gather.13.cloned.1.call-done) | copy-start | bytes 9437188
  842.0 11.1 %slice-start.6 = ((s8[12582912]{0:T(1024)(128)(4,1)}), s8[4194304]{0:T(1024)(128)(4,1)S(1)}, s32[]{:S(2)}) async-start(s8[12582912]{0:T(1024)(128)(4,1)} %bitcast.476), calls=%async_computation.22 | async-start | bytes 8388608
  842.1 11.0 %slice-start.7 = ((s8[12582912]{0:T(1024)(128)(4,1)}), s8[4194304]{0:T(1024)(128)(4,1)S(1)}, s32[]{:S(2)}) async-start(s8[12582912]{0:T(1024)(128)(4,1)} %bitcast.476), calls=%async_computation.23 | async-start | bytes 8388608
  842.1 11.0 %slice-start.8 = ((s8[12582912]{0:T(1024)(128)(4,1)}), s8[4194304]{0:T(1024)(128)(4,1)S(1)}, s32[]{:S(2)}) async-start(s8[12582912]{0:T(1024)(128)(4,1)} %bitcast.476), calls=%async_computation.24 | async-start | bytes 8388608
  (47 other events, 202.0 us)
Sparse Core Ops, SparseCore 0:
  21.0 92.0 all-gather.26
  114.7 87.8 all-gather.22
  204.2 87.8 all-gather.20
  293.5 87.8 all-gather.24
  550.1 60.1 all-gather.14
  616.6 60.1 all-gather.12
  689.8 60.0 all-gather.18
  792.1 60.0 all-gather.16
